TPU v7x, 32 devices: a whole 2x2x4 slice. The times are simulated.
32 devices in a mesh: grp: 2 (over y), ctx: 4 (over z), tp: 4 (over x, core).
Axes of the slice: x: 2, y: 2, z: 4, core: 2. Of those that a mesh axis runs over, the one named last changes fastest.
Arguments:
- query_projected: bfloat16 [1536, 2048], P(('grp', 'ctx'), 'tp'), parts along dimension 0, may hold values from -6 to 6
- key_projected: bfloat16 [1536, 2048], P(('grp', 'ctx'), 'tp'), parts along dimension 0, may hold values from -6 to 6
- value_projected: bfloat16 [1536, 2048], P(('grp', 'ctx'), 'tp'), parts along dimension 0, may hold values from -6 to 6
- long_conv_output: bfloat16 [1536, 2048], P(('grp', 'ctx'), 'tp'), parts along dimension 0, may hold values from -6 to 6
- short_conv_filter: float32 [3, 3, 2048], P(None, None, 'tp'), may hold values from -3.5 to 3.5
- direct_bias: float32 [2048], P('tp'), may hold values from -3 to 3
- mode_residue: float32 [2048, 16], P('tp'), may hold values from -1.5 to 1.5
- mode_decay_rate: float32 [2048, 16], P('tp'), may hold values from 0.5 to 25
- output_weight: bfloat16 [2048, 2048], P(None, 'tp'), may hold values from -0.125 to 0.125
- adapter_down_factor: bfloat16 [2048, 16], replicated, may hold values from -0.125 to 0.125
- adapter_up_factor: bfloat16 [16, 2048], P(None, 'tp'), may hold values from -0.125 to 0.125
- output_gradient: bfloat16 [1536, 2048], P(('grp', 'ctx'), 'tp'), parts along dimension 0, may hold values from -6 to 6
Outputs:
- query_input_gradient: bfloat16 [1536, 2048], P(('grp', 'ctx'), 'tp'), parts along dimension 0
- key_input_gradient: bfloat16 [1536, 2048], P(('grp', 'ctx'), 'tp'), parts along dimension 0
- value_input_gradient: bfloat16 [1536, 2048], P(('grp', 'ctx'), 'tp'), parts along dimension 0
- down_factor_gradient: float32 [4096, 16], P(('grp', 'tp')), parts along dimension 0
- up_factor_gradient: float32 [32, 2048], P('grp', 'tp'), parts along dimension 0
There are 2 independent parts, one for each index of `grp`. A program takes and returns all parts, laid end to end along the dimension named above; an argument that names none is the same for every part. Nothing has to cross between parts.
All inputs are finite; a program needn't handle non-finite values.
Results may differ from a plain program's by a relative error of at most 0.013.
Values may be sent and summed in bfloat16 or wider, within the bound.
A program may use at most 64 MiB of HBM per device.

v0:
```python
import math

import jax
import jax.numpy as jnp
from jax import lax
from jax.sharding import PartitionSpec as P

FA = 128


adapter_scale = 2.0
highest = lax.Precision.HIGHEST


def passed_along(value, axis, by):
    peers = lax.axis_size(axis)
    pairs = [(i, i + by) for i in range(peers) if 0 <= i + by < peers]
    return lax.ppermute(value, axis, pairs)


def contract_final_axis(left, right):
    return lax.dot_general(
        left, right, (((1,), (1,)), ((), ())), preferred_element_type=jnp.float32
    )


def contract_first(left, right):
    return lax.dot_general(
        left, right, (((0,), (0,)), ((), ())), preferred_element_type=jnp.float32
    )


def delayed_taps(signal, before, taps):
    length = signal.shape[0]
    joined = jnp.concatenate([before, signal], axis=0)
    return taps[0] * joined[2:] + taps[1] * joined[1 : length + 1] + taps[2] * joined[0:length]


def advanced_taps(signal, after, taps):
    length = signal.shape[0]
    joined = jnp.concatenate([signal, after], axis=0)
    return taps[0] * joined[0:length] + taps[1] * joined[1 : length + 1] + taps[2] * joined[2:]


def square_table(order):
    counter = jnp.arange(order, dtype=jnp.int32)
    angle = (counter[:, None] * counter[None, :] % order).astype(jnp.float32) * (
        2.0 * math.pi / order
    )
    return (jnp.cos(angle), jnp.sin(angle))


def twiddle_table(first_size, second_size):
    total_size = first_size * second_size
    product = (
        jnp.arange(first_size, dtype=jnp.int32)[:, None]
        * jnp.arange(second_size, dtype=jnp.int32)[None, :]
    )
    angle = (product % total_size).astype(jnp.float32) * (2.0 * math.pi / total_size)
    return (jnp.cos(angle), jnp.sin(angle))


def forward_spectrum(signal, tables):
    cos_first, sin_first, cos_second, sin_second, cos_twist, sin_twist = tables
    half_rows = signal.shape[1]
    section_re = jnp.einsum("ka,cab->ckb", cos_first[:, :half_rows], signal, precision=highest)
    section_im = -jnp.einsum("ka,cab->ckb", sin_first[:, :half_rows], signal, precision=highest)
    twist_re = section_re * cos_twist + section_im * sin_twist
    twist_im = section_im * cos_twist - section_re * sin_twist
    spec_re = jnp.einsum("ckb,bj->ckj", twist_re, cos_second, precision=highest) + jnp.einsum(
        "ckb,bj->ckj", twist_im, sin_second, precision=highest
    )
    spec_im = jnp.einsum("ckb,bj->ckj", twist_im, cos_second, precision=highest) - jnp.einsum(
        "ckb,bj->ckj", twist_re, sin_second, precision=highest
    )
    return (spec_re, spec_im)


def inverse_half(spec_re, spec_im, tables, half_rows, total_size):
    cos_first, sin_first, cos_second, sin_second, cos_twist, sin_twist = tables
    back_re = jnp.einsum("ckj,jb->ckb", spec_re, cos_second, precision=highest) - jnp.einsum(
        "ckj,jb->ckb", spec_im, sin_second, precision=highest
    )
    back_im = jnp.einsum("ckj,jb->ckb", spec_im, cos_second, precision=highest) + jnp.einsum(
        "ckj,jb->ckb", spec_re, sin_second, precision=highest
    )
    turned_re = back_re * cos_twist - back_im * sin_twist
    turned_im = back_im * cos_twist + back_re * sin_twist
    result = jnp.einsum(
        "ak,ckb->cab", cos_first[:half_rows], turned_re, precision=highest
    ) - jnp.einsum("ak,ckb->cab", sin_first[:half_rows], turned_im, precision=highest)
    return result / total_size


def filter_time(residue, rate, sequence_length):
    times = jnp.arange(sequence_length, dtype=jnp.int32).astype(jnp.float32)
    weights = residue * jnp.sqrt(rate / sequence_length)

    def add_mode(index_mode, total):
        rate_now = lax.dynamic_slice_in_dim(rate, index_mode, 1, 1)
        weight_now = lax.dynamic_slice_in_dim(weights, index_mode, 1, 1)
        return total + weight_now * jnp.exp(-(rate_now * times[None, :]) / sequence_length)

    start = jnp.zeros((residue.shape[0], sequence_length), jnp.float32)
    return lax.fori_loop(0, residue.shape[1], add_mode, start)


def on_device(
    query_projected,
    key_projected,
    value_projected,
    long_conv_output,
    short_conv_filter,
    direct_bias,
    mode_residue,
    mode_decay_rate,
    output_weight,
    adapter_down_factor,
    adapter_up_factor,
    output_gradient,
):
    tok_rows = query_projected.shape[0]
    channel_slice = query_projected.shape[1]
    ctx_count = lax.axis_size("ctx")
    ctx_rank = lax.axis_index("ctx")
    tensor_parallel_rank = lax.axis_index("tp")
    sequence_length = tok_rows * ctx_count
    chan_each = channel_slice // ctx_count
    first_size = FA
    second_size = 2 * sequence_length // first_size
    half_rows = first_size // 2
    tails = jnp.stack(
        [
            query_projected[tok_rows - 2 :],
            key_projected[tok_rows - 2 :],
            value_projected[tok_rows - 2 :],
        ]
    )
    before = passed_along(tails, "ctx", 1).astype(jnp.float32)
    query = delayed_taps(query_projected.astype(jnp.float32), before[0], short_conv_filter[0])
    key_act = delayed_taps(key_projected.astype(jnp.float32), before[1], short_conv_filter[1])
    value_act = delayed_taps(value_projected.astype(jnp.float32), before[2], short_conv_filter[2])
    conv_value = long_conv_output.astype(jnp.float32)
    gated_signal = (query * conv_value).astype(jnp.bfloat16)
    down_factor_slice = lax.dynamic_slice_in_dim(
        adapter_down_factor, tensor_parallel_rank * channel_slice, channel_slice, 0
    )
    adapter_portion = contract_final_axis(output_gradient, adapter_up_factor)
    act_part = jnp.dot(gated_signal, down_factor_slice, preferred_element_type=jnp.float32)
    adapter_sum, act_sum = lax.psum((adapter_portion, act_part), "tp")
    adapter_gradient = adapter_sum.astype(jnp.bfloat16)
    adapter_activation = act_sum.astype(jnp.bfloat16)
    partial_value = contract_final_axis(output_gradient, output_weight).astype(jnp.bfloat16)
    summed = lax.psum(partial_value, "tp").astype(jnp.float32)
    gate_total = lax.dynamic_slice_in_dim(
        summed, tensor_parallel_rank * channel_slice, channel_slice, 1
    )
    gate_gradient = gate_total + adapter_scale * contract_final_axis(
        adapter_gradient, down_factor_slice
    )
    query_grad = gate_gradient * conv_value
    conv_grad = gate_gradient * query
    outgoing = conv_grad.T.reshape(ctx_count, chan_each, tok_rows)
    incoming = lax.all_to_all(
        outgoing.astype(jnp.bfloat16), "ctx", split_axis=0, concat_axis=2, tiled=True
    ).astype(outgoing.dtype)
    signal = incoming.reshape(chan_each, half_rows, second_size)
    residue_local = lax.dynamic_slice_in_dim(mode_residue, ctx_rank * chan_each, chan_each, 0)
    rate_local = lax.dynamic_slice_in_dim(mode_decay_rate, ctx_rank * chan_each, chan_each, 0)
    cos_first, sin_first = square_table(first_size)
    cos_second, sin_second = square_table(second_size)
    cos_twist, sin_twist = twiddle_table(first_size, second_size)
    tables = (cos_first, sin_first, cos_second, sin_second, cos_twist, sin_twist)
    filter_taps = filter_time(residue_local, rate_local, sequence_length)
    filt_re, filt_im = forward_spectrum(
        filter_taps.reshape(chan_each, half_rows, second_size), tables
    )
    grad_re, grad_im = forward_spectrum(signal, tables)
    prod_re = grad_re * filt_re + grad_im * filt_im
    prod_im = grad_im * filt_re - grad_re * filt_im
    long_corr = inverse_half(prod_re, prod_im, tables, half_rows, 2 * sequence_length)
    returned = lax.all_to_all(
        long_corr.reshape(1, chan_each, sequence_length).astype(jnp.bfloat16),
        "ctx",
        split_axis=2,
        concat_axis=0,
        tiled=True,
    ).astype(jnp.float32)
    corr_tokens = returned.reshape(channel_slice, tok_rows).T
    inner_grad = corr_tokens + direct_bias * conv_grad
    key_grad = inner_grad * value_act
    value_grad = inner_grad * key_act
    heads = jnp.stack([query_grad[:2], key_grad[:2], value_grad[:2]])
    after = passed_along(heads, "ctx", -1)
    query_input_gradient = advanced_taps(query_grad, after[0], short_conv_filter[0]).astype(
        jnp.bfloat16
    )
    key_input_gradient = advanced_taps(key_grad, after[1], short_conv_filter[1]).astype(
        jnp.bfloat16
    )
    value_input_gradient = advanced_taps(value_grad, after[2], short_conv_filter[2]).astype(
        jnp.bfloat16
    )
    down_part = contract_first(gated_signal, adapter_gradient)
    up_part = contract_first(adapter_activation, output_gradient)
    down_factor_sum, up_factor_sum = lax.psum((down_part, up_part), "ctx")
    down_factor_gradient = adapter_scale * down_factor_sum / math.sqrt(sequence_length)
    up_factor_gradient = adapter_scale * up_factor_sum / math.sqrt(sequence_length)
    return (
        query_input_gradient,
        key_input_gradient,
        value_input_gradient,
        down_factor_gradient,
        up_factor_gradient,
    )


def solution(mesh):
    in_specs = (
        P(("grp", "ctx"), "tp"),
        P(("grp", "ctx"), "tp"),
        P(("grp", "ctx"), "tp"),
        P(("grp", "ctx"), "tp"),
        P(None, None, "tp"),
        P("tp"),
        P("tp", None),
        P("tp", None),
        P(None, "tp"),
        P(),
        P(None, "tp"),
        P(("grp", "ctx"), "tp"),
    )
    out_specs = (
        P(("grp", "ctx"), "tp"),
        P(("grp", "ctx"), "tp"),
        P(("grp", "ctx"), "tp"),
        P(("grp", "tp"), None),
        P("grp", "tp"),
    )
    return jax.shard_map(
        on_device, mesh=mesh, in_specs=in_specs, out_specs=out_specs, check_vma=False
    )
```

profile of v0, /device:TPU:0, one launch (start us, length us, event | category | flops | bytes accessed | tf_op | source)
XLA Modules:
  0.0 162.3 jit_solution(12655223299389047023)
XLA Ops:
  8.1 0.8 slice_bitcast_fusion.21
  8.9 0.7 slice_bitcast_fusion.19
  9.7 0.6 pad_maximum_fusion.7
  10.3 5.5 %collective-permute-start = (bf16[3,2,512]{2,1,0:T(2,128)(2,1)}, bf16[3,2,512]{2,1,0:T(2,128)(2,1)}, u32[]{:S(2)}, u32[]{:S(2)}) collective-permute-start(bf16[3,2,512]{2,1,0:T(2,128)(2,1)} %pad_maximum_fusion.7), channel_id=1, source_target_pairs={{0,4},{4,8},{8,12},{1,5},{5,9},{9,13},{2,6},{6,10},{10,14},{3,7},{... | collective-permute-start | bytes 18440 | tf_op jit(solution)/shard_map/ppermute | solution.py:18
  15.8 2.7 %convolution_convert_fusion = bf16[192,2048]{1,0:T(8,128)(2,1)} fusion(bf16[192,512]{1,0:T(8,128)(2,1)} %param.25, bf16[2048,512]{1,0:T(8,128)(2,1)S(1)} %copy-done), kind=kOutput, calls=%fused_computation.5 | convolution fusion | flops 403046400 | bytes 3080192 | tf_op jit(solution)/shard_map/dot_general | solution.py:22
  18.5 0.3 fusion.79
  18.8 0.6 fusion.207
  19.6 0.8 constant_dynamic-slice_fusion
  20.3 3.6 %while.14 = (s32[]{:T(128)}, f32[128,768]{1,0:T(8,128)S(1)}, f32[128,16]{0,1:T(8,128)S(1)}, f32[128,16]{0,1:T(8,128)S(1)}, s32[]{:T(128)}, /*index=5*/s32[]{:T(128)}) while((s32[]{:T(128)}, f32[128,768]{1,0:T(8,128)S(1)}, f32[128,16]{0,1:T(8,128)S(1)}, f32[128,16]{0,1:T(8,128)S(1)}, s32[]{:T(128)}, /*index=5*/s32[]{:T(128)}) %tuple.61), condition=%wide.region_3.4_spmd.clone, body=%wide.region_2.0_spmd.clone.sunk | while | flops 590595 | bytes 795731 | solution.py:105
  20.8 0.2 select_add_fusion.2
  24.0 0.9 copy.60
  24.9 1.0 reshape.91
  25.9 2.3 %convolution_bitcast_fusion = f32[128,128,12]{1,0,2:T(8,128)} fusion(f32[128,64,12]{0,2,1:T(8,128)S(1)} %reshape.91, f32[128,128]{0,1:T(8,128)S(1)} %fusion.79), kind=kOutput, calls=%fused_computation.12 | convolution fusion | flops 150994944 | bytes 1343488 | tf_op jit(solution)/shard_map/ka,cab->ckb/dot_general | solution.py:66
  28.2 0.3 fusion.78
  28.5 0.8 convert_element_type.154
  29.3 0.7 convert_element_type.155
  30.0 0.6 slice_bitcast_fusion.14
  30.6 1.5 fusion.55
  32.1 0.9 fusion.80
  33.0 11.4 %all-reduce = (bf16[192,16]{0,1:T(8,128)(2,1)}, bf16[192,16]{0,1:T(8,128)(2,1)}) all-reduce(f32[192,16]{0,1:T(8,128)S(1)} %fusion.208, f32[192,16]{0,1:T(8,128)S(1)} %fusion.80), channel_id=1, replica_groups=mesh['grp'=2,'ctx'=4,'tp'=4] {'tp'}, use_global_device_ids=true, to_apply=%region_1.0 | all-reduce | flops 6144 | bytes 36864 | tf_op jit(solution)/shard_map/psum | solution.py:150
  44.4 8.6 %all-reduce.5.cloned.1.call-done = bf16[192,2048]{1,0:T(8,128)(2,1)} async-done(((bf16[192,2048]{1,0:T(8,128)(2,1)}), bf16[192,2048]{1,0:T(8,128)(2,1)}) %all-reduce.5.cloned.1.call-update) | async-done | bytes 786448 | tf_op jit(solution)/shard_map/psum | solution.py:154
  52.9 1.2 fusion.4
  54.1 0.7 copy_bitcast_fusion
  54.9 4.6 %all-to-all-start = ((bf16[4,128,192]{1,2,0:T(8,128)(2,1)}), bf16[4,128,192]{1,2,0:T(8,128)(2,1)}, u32[]{:S(2)}, u32[]{:S(2)}) async-start(bf16[4,128,192]{1,2,0:T(8,128)(2,1)} %copy_bitcast_fusion), calls=%async_computation | async-start | bytes 393216 | tf_op jit(solution)/shard_map/all_to_all | solution.py:164
  59.5 1.7 %fusion.163 = f32[512,16]{0,1:T(8,128)} fusion(bf16[192,16]{0,1:T(8,128)(2,1)} %get-tuple-element.125, f32[192,512]{1,0:T(8,128)S(1)} %fusion.55, bf16[192,512]{1,0:T(8,128)(2,1)} %param.17), kind=kOutput, calls=%fused_computation.210 | convolution fusion | flops 3440640 | bytes 628736 | tf_op jit(solution)/shard_map/dot_general | solution.py:28
  61.2 4.8 %all-to-all-done = bf16[4,128,192]{1,2,0:T(8,128)(2,1)} async-done(((bf16[4,128,192]{1,2,0:T(8,128)(2,1)}), bf16[4,128,192]{1,2,0:T(8,128)(2,1)}, u32[]{:S(2)}, u32[]{:S(2)}) %all-to-all-start) | async-done | bytes 196640 | tf_op jit(solution)/shard_map/all_to_all | solution.py:164
  66.0 1.7 %reshape.90 = bf16[128,64,12]{0,2,1:T(8,128)(2,1)} reshape(bf16[1,128,4,192]{1,3,2,0:T(8,128)(2,1)} %bitcast.10) | data formatting | bytes 393216 | tf_op jit(solution)/shard_map/reshape | solution.py:167
  67.7 1.6 convolution_bitcast_fusion.1
  69.3 1.5 fusion.3
  70.8 1.6 multiply_add_fusion.1
  72.4 1.6 fusion.12
  74.0 1.6 fusion.8
  75.6 1.7 %convolution_add_fusion = f32[128,128,12]{1,2,0:T(8,128)S(1)} fusion(f32[128,128,12]{1,2,0:T(8,128)S(1)} %fusion.12, f32[128,128,12]{1,0,2:T(8,128)S(1)} %get-tuple-element.136), kind=kOutput, calls=%fused_computation.8 | convolution fusion | flops 28509456 | bytes 2359296 | tf_op jit(solution)/shard_map/ckb,bj->ckj/dot_general | solution.py:70
  77.3 1.6 fusion.18
  78.9 1.6 fusion.14
  80.6 1.6 %convolution_add_fusion.1 = f32[128,128,12]{1,2,0:T(8,128)S(1)} fusion(f32[128,128,12]{1,2,0:T(8,128)S(1)} %fusion.18, f32[128,128,12]{1,0,2:T(8,128)S(1)} %get-tuple-element.152), kind=kOutput, calls=%fused_computation.9 | convolution fusion | flops 28509456 | bytes 2359296 | tf_op jit(solution)/shard_map/ckb,bj->ckj/dot_general | solution.py:70
  82.2 1.9 %convolution_subtract_fusion = f32[128,128,12]{1,2,0:T(8,128)S(1)} fusion(f32[128,128,12]{1,2,0:T(8,128)S(1)} %fusion.8, f32[128,128,12]{1,0,2:T(8,128)S(1)} %get-tuple-element.135), kind=kOutput, calls=%fused_computation.6 | convolution fusion | flops 28509456 | bytes 2359296 | tf_op jit(solution)/shard_map/ckb,bj->ckj/dot_general | solution.py:73
  84.1 2.0 %multiply_add_fusion = (f32[128,128,12]{1,2,0:T(8,128)S(1)}, f32[128,128,12]{1,2,0:T(8,128)S(1)}) fusion(f32[128,128,12]{1,2,0:T(8,128)S(1)} %convolution_subtract_fusion, f32[128,128,12]{1,2,0:T(8,128)S(1)} %convolution_add_fusion.1, f32[128,128,12]{1,2,0:T(8,128)S(1)} %convolution_add_fusion, f32[128,128,12]{1,2,0:T(8,128)S(1)} %fusion.14, ...), kind=kOutput, calls=%fused_computation.35 | convolution fusion | flops 29689104 | bytes 5505024 | tf_op jit(solution)/shard_map/ckb,bj->ckj/dot_general | solution.py:73
  86.1 1.0 fusion.89
  87.1 1.0 fusion.95
  88.2 1.0 fusion.87
  89.2 1.0 fusion.97
  90.3 2.0 %fusion.23 = f32[128,12,64]{0,2,1:T(8,128)S(1)} fusion(f32[128,12]{0,1:T(8,128)S(1)} %get-tuple-element.161, f32[128,12]{0,1:T(8,128)S(1)} %get-tuple-element.162, f32[128,128]{0,1:T(8,128)S(1)} %fusion.79, f32[128,128,12]{1,2,0:T(8,128)S(1)} %fusion.89, f32[128,128,12]{1,2,0:T(8,128)S(1)} %fusion.97, f32[128,128,12]{1,2,0:T(8,128)S(1)} %fusion.87, ...), kind=kOutput, calls=%fused_computation.41 | convolution fusion | flops 151977984 | bytes 3616768 | tf_op jit(solution)/shard_map/ak,ckb->cab/dot_general | solution.py:89
  92.3 2.1 %fusion.7 = bf16[128,64,12]{0,1,2:T(8,128)(2,1)S(1)} fusion(f32[128,12,64]{0,2,1:T(8,128)S(1)} %fusion.23, f32[128,12]{0,1:T(8,128)S(1)} %get-tuple-element.161, f32[128,12]{0,1:T(8,128)S(1)} %get-tuple-element.162, f32[128,128]{0,1:T(8,128)S(1)} %fusion.78, f32[128,128,12]{1,2,0:T(8,128)S(1)} %fusion.89, f32[128,128,12]{1,2,0:T(8,128)S(1)} %fusion.97, ...), kind=kOutput, calls=%fused_computation.21 | convolution fusion | flops 152272896 | bytes 3813376 | tf_op jit(solution)/shard_map/ak,ckb->cab/dot_general | solution.py:91
  94.5 0.9 convert_element_type.180
  95.4 0.5 broadcast.87
  95.9 3.0 %reduce = bf16[768,128]{1,0:T(8,128)(2,1)S(1)} reduce(bf16[768,1,128]{2,1,0:T(2,128)(2,1)} %bitcast.143, bf16[]{:T(256)} %broadcast.87), dimensions={1}, to_apply=%bitcast.119.reduce_sub_computation | reduce | bytes 393218
  98.9 0.7 reshape.100
  99.6 4.0 %all-to-all-start.1 = ((bf16[4,2,12288]{2,1,0:T(2,128)(2,1)}), bf16[4,2,12288]{2,1,0:T(2,128)(2,1)}, u32[]{:S(2)}, u32[]{:S(2)}) async-start(bf16[4,2,12288]{2,1,0:T(2,128)(2,1)} %reshape.100), calls=%async_computation.1 | async-start | bytes 393216 | tf_op jit(solution)/shard_map/all_to_all | solution.py:182
  103.8 0.8 fusion.209
  104.6 1.7 %convert_element_type.169 = f32[192,512]{1,0:T(8,128)} convert(bf16[192,512]{1,0:T(8,128)(2,1)} %param.16) | non-fusion elementwise | flops 98304 | bytes 589824 | tf_op jit(solution)/shard_map/convert_element_type | solution.py:142
  106.3 1.7 %convert_element_type.170 = f32[192,512]{1,0:T(8,128)} convert(bf16[192,512]{1,0:T(8,128)(2,1)} %param.15) | non-fusion elementwise | flops 98304 | bytes 589824 | tf_op jit(solution)/shard_map/convert_element_type | solution.py:141
  108.0 34.4 %all-reduce.7.cloned.1.call-done = (f32[512,16]{0,1:T(8,128)}, f32[16,512]{1,0:T(8,128)}) async-done(((f32[512,16]{0,1:T(8,128)}, f32[16,512]{1,0:T(8,128)}), (f32[512,16]{0,1:T(8,128)}, f32[16,512]{1,0:T(8,128)})) %all-reduce.7.cloned.1.call-update) | async-done | bytes 65552 | tf_op jit(solution)/shard_map/psum | solution.py:206
  142.4 1.4 broadcast_multiply_fusion
  143.7 1.6 reshape.101
  145.5 0.3 copy.78
  145.8 0.5 copy-done.7
  146.3 0.2 fusion.51
  146.8 1.3 collective-permute-start.1
  148.1 0.6 broadcast_multiply_fusion.1
  148.7 3.7 %collective-permute-done.1 = f32[3,2,512]{2,1,0:T(2,128)S(1)} collective-permute-done((f32[3,2,512]{2,1,0:T(2,128)S(1)}, f32[3,2,512]{2,1,0:T(2,128)S(1)}, u32[]{:S(2)}, u32[]{:S(2)}) %collective-permute-start.1) | collective-permute-done | bytes 12320 | tf_op jit(solution)/shard_map/ppermute | solution.py:18
  152.4 0.8 fusion.31
  153.2 0.8 fusion.36
  154.0 0.8 fusion.41
  (114 shorter events, 3.6 us)
Async XLA Ops:
  8.0 7.8 %copy-start = (bf16[2048,512]{1,0:T(8,128)(2,1)S(1)}, bf16[2048,512]{1,0:T(8,128)(2,1)}, u32[]{:S(2)}) copy-start(bf16[2048,512]{1,0:T(8,128)(2,1)} %param.22) | copy-start | bytes 6291460
  8.0 11.4 %copy-start.2 = (bf16[192,512]{1,0:T(8,128)(2,1)S(1)}, bf16[192,512]{1,0:T(8,128)(2,1)}, u32[]{:S(2)}) copy-start(bf16[192,512]{1,0:T(8,128)(2,1)} %param.25) | copy-start | bytes 589828
  8.0 10.7 %copy-start.22 = (f32[3,3,512]{2,1,0:T(4,128)S(1)}, f32[3,3,512]{2,1,0:T(4,128)}, u32[]{:S(2)}) copy-start(f32[3,3,512]{2,1,0:T(4,128)} %param.18) | copy-start | bytes 55300
  8.0 11.4 %copy-start.21 = (bf16[16,512]{1,0:T(8,128)(2,1)S(1)}, bf16[16,512]{1,0:T(8,128)(2,1)}, u32[]{:S(2)}) copy-start(bf16[16,512]{1,0:T(8,128)(2,1)} %param.24) | copy-start | bytes 49156
  8.0 44.9 %all-reduce.5.cloned.1.call-start = ((), (), s32[]{:S(2)}) async-start(), calls=%async_computation.2 | async-start | bytes 1572864 | tf_op jit(solution)/shard_map/psum | solution.py:154
  10.3 19.0 %collective-permute-start = (bf16[3,2,512]{2,1,0:T(2,128)(2,1)}, bf16[3,2,512]{2,1,0:T(2,128)(2,1)}, u32[]{:S(2)}, u32[]{:S(2)}) collective-permute-start(bf16[3,2,512]{2,1,0:T(2,128)(2,1)} %pad_maximum_fusion.7), channel_id=1, source_target_pairs={{0,4},{4,8},{8,12},{1,5},{5,9},{9,13},{2,6},{6,10},{10,14},{3,7},{... | collective-permute-start | bytes 18440 | tf_op jit(solution)/shard_map/ppermute | solution.py:18
  23.9 4.5 %copy-start.8 = (bf16[192,512]{1,0:T(8,128)(2,1)S(1)}, bf16[192,512]{1,0:T(8,128)(2,1)}, u32[]{:S(2)}) copy-start(bf16[192,512]{1,0:T(8,128)(2,1)} %param.14) | copy-start | bytes 589828
  23.9 8.1 %copy-start.4 = (bf16[192,512]{1,0:T(8,128)(2,1)S(1)}, bf16[192,512]{1,0:T(8,128)(2,1)}, u32[]{:S(2)}) copy-start(bf16[192,512]{1,0:T(8,128)(2,1)} %param.17) | copy-start | bytes 589828
  54.9 11.2 %all-to-all-start = ((bf16[4,128,192]{1,2,0:T(8,128)(2,1)}), bf16[4,128,192]{1,2,0:T(8,128)(2,1)}, u32[]{:S(2)}, u32[]{:S(2)}) async-start(bf16[4,128,192]{1,2,0:T(8,128)(2,1)} %copy_bitcast_fusion), calls=%async_computation | async-start | bytes 393216 | tf_op jit(solution)/shard_map/all_to_all | solution.py:164
  67.7 3.1 %copy-start.1 = (f32[128,128,12]{1,0,2:T(8,128)S(1)}, f32[128,128,12]{1,0,2:T(8,128)}, u32[]{:S(2)}) copy-start(f32[128,128,12]{1,0,2:T(8,128)} %convolution_bitcast_fusion) | copy-start | bytes 2359300
  94.4 9.4 %copy-start.3 = (bf16[192,512]{1,0:T(8,128)(2,1)S(1)}, bf16[192,512]{1,0:T(8,128)(2,1)}, u32[]{:S(2)}) copy-start(bf16[192,512]{1,0:T(8,128)(2,1)} %param.25) | copy-start | bytes 589828
  94.4 9.4 %copy-start.23 = (bf16[192,16]{0,1:T(8,128)(2,1)S(1)}, bf16[192,16]{0,1:T(8,128)(2,1)}, u32[]{:S(2)}) copy-start(bf16[192,16]{0,1:T(8,128)(2,1)} %get-tuple-element.126) | copy-start | bytes 18436
  99.6 44.1 %all-to-all-start.1 = ((bf16[4,2,12288]{2,1,0:T(2,128)(2,1)}), bf16[4,2,12288]{2,1,0:T(2,128)(2,1)}, u32[]{:S(2)}, u32[]{:S(2)}) async-start(bf16[4,2,12288]{2,1,0:T(2,128)(2,1)} %reshape.100), calls=%async_computation.1 | async-start | bytes 393216 | tf_op jit(solution)/shard_map/all_to_all | solution.py:182
  103.6 42.1 %copy-start.5 = (bf16[192,512]{1,0:T(8,128)(2,1)S(1)}, bf16[192,512]{1,0:T(8,128)(2,1)}, u32[]{:S(2)}) copy-start(bf16[192,512]{1,0:T(8,128)(2,1)} %param.17) | copy-start | bytes 589828
  103.6 42.1 %copy-start.16 = (f32[1,1,512]{2,1,0:T(1,128)S(1)}, f32[1,1,512]{2,1,0:T(1,128)}, u32[]{:S(2)}) copy-start(f32[1,1,512]{2,1,0:T(1,128)} %get-tuple-element.143) | copy-start | bytes 6148
  103.7 42.1 %copy-start.17 = (f32[1,1,512]{2,1,0:T(1,128)S(1)}, f32[1,1,512]{2,1,0:T(1,128)}, u32[]{:S(2)}) copy-start(f32[1,1,512]{2,1,0:T(1,128)} %get-tuple-element.144) | copy-start | bytes 6148
  103.7 42.1 %copy-start.18 = (f32[1,1,512]{2,1,0:T(1,128)S(1)}, f32[1,1,512]{2,1,0:T(1,128)}, u32[]{:S(2)}) copy-start(f32[1,1,512]{2,1,0:T(1,128)} %get-tuple-element.145) | copy-start | bytes 6148
  103.7 42.1 %copy-start.20 = (f32[2,512]{1,0:T(2,128)S(1)}, f32[2,512]{1,0:T(2,128)}, u32[]{:S(2)}) copy-start(f32[2,512]{1,0:T(2,128)} %get-tuple-element.157) | copy-start | bytes 12292
  103.7 42.1 %copy-start.24 = (f32[512]{0:T(512)S(1)}, f32[512]{0:T(512)}, u32[]{:S(2)}) copy-start(f32[512]{0:T(512)} %param.19) | copy-start | bytes 6148
  103.7 38.7 %all-reduce.7.cloned.1.call-start = ((), (), s32[]{:S(2)}) async-start(), calls=%async_computation.3 | async-start | bytes 131072 | tf_op jit(solution)/shard_map/psum | solution.py:206
  145.3 1.0 copy-start.7
  145.4 1.2 copy-start.6
  145.4 1.2 copy-start.13
  145.4 1.2 copy-start.14
  145.4 1.2 copy-start.15
  145.4 1.2 copy-start.19
  146.3 1.8 %copy-start.9 = (f32[512,16]{0,1:T(8,128)S(1)}, f32[512,16]{0,1:T(8,128)}, u32[]{:S(2)}) copy-start(f32[512,16]{0,1:T(8,128)} %get-tuple-element.127) | copy-start | bytes 98308
  146.3 7.7 %copy-start.10 = (f32[1,1,512]{2,1,0:T(1,128)S(1)}, f32[1,1,512]{2,1,0:T(1,128)}, u32[]{:S(2)}) copy-start(f32[1,1,512]{2,1,0:T(1,128)} %get-tuple-element.146) | copy-start | bytes 6148
  146.3 7.7 %copy-start.11 = (f32[1,1,512]{2,1,0:T(1,128)S(1)}, f32[1,1,512]{2,1,0:T(1,128)}, u32[]{:S(2)}) copy-start(f32[1,1,512]{2,1,0:T(1,128)} %get-tuple-element.147) | copy-start | bytes 6148
  146.3 7.7 %copy-start.12 = (f32[1,1,512]{2,1,0:T(1,128)S(1)}, f32[1,1,512]{2,1,0:T(1,128)}, u32[]{:S(2)}) copy-start(f32[1,1,512]{2,1,0:T(1,128)} %get-tuple-element.148) | copy-start | bytes 6148
  146.8 5.6 %collective-permute-start.1 = (f32[3,2,512]{2,1,0:T(2,128)S(1)}, f32[3,2,512]{2,1,0:T(2,128)S(1)}, u32[]{:S(2)}, u32[]{:S(2)}) collective-permute-start(f32[3,2,512]{2,1,0:T(2,128)S(1)} %pad_maximum_fusion.6), channel_id=1, source_target_pairs={{4,0},{8,4},{12,8},{5,1},{9,5},{13,9},{6,2},{10,6},{14,10},{7,3},{... | collective-permute-start | bytes 36872 | tf_op jit(solution)/shard_map/ppermute | solution.py:18
Sparse Core Ops, SparseCore 0:
  18.6 34.2 all-reduce.4
Sparse Core Ops, SparseCore 1:
  107.1 35.2 all-reduce.6
where the time goes:
time: 163 us; the launch traced here: 162 us
  waiting for transfers between devices  51.4 us (32%)
  matrix products  36.2 us (22%)
  other arithmetic  19.7 us (12%)
  between operations  16.1 us (10%)
  starting transfers between devices  15.5 us (10%)
  local copies, waits for them, and re-layouts  11.4 us (7%)
  blocking collectives  11.4 us (7%)
    psum x1, waiting for transfers between devices, on_device(): down_factor_sum, up_factor_sum = lax.psum((down_part, up_part), 'ctx')  34.4 us
    psum x1, blocking collectives, on_device(): adapter_sum, act_sum = lax.psum((adapter_portion, act_part), 'tp')  11.4 us
    psum x1, waiting for transfers between devices, on_device(): summed = lax.psum(partial_value, 'tp').astype(jnp.float32)  8.55 us
    ppermute x2, starting transfers between devices, passed_along(): return lax.ppermute(value, axis, pairs)  6.8 us
    all_to_all x1, waiting for transfers between devices, on_device(): lax.all_to_all(outgoing.astype(jnp.bfloat16), 'ctx', split_axis=0, concat...  4.78 us
    all_to_all x1, starting transfers between devices, on_device(): lax.all_to_all(outgoing.astype(jnp.bfloat16), 'ctx', split_axis=0, concat...  4.6 us
    dot_general x3, matrix products, contract_final_axis(): lax.dot_general(left, right, (((1,), (1,)), ((), ())), preferred_element_...  4 us
    all_to_all x1, starting transfers between devices, on_device(): lax.all_to_all(long_corr.reshape(1, chan_each, sequence_length).astype(jn...  4 us
  transfers between devices with their start and end apart: 6, of which 4 were waited for; matrix products, arithmetic and copies ran while one was open for 15% of the time, Pallas kernels for 0%

commit v1 on v0

v1 whole, which is shorter than its diff:
```python
import functools
import math

import jax
import jax.numpy as jnp
from jax import lax
from jax.experimental import pallas as pl
from jax.experimental.pallas import tpu as pltpu
from jax.sharding import PartitionSpec as P

adapter_scale = 2.0
MESH = pl.DeviceIdType.MESH
SEGMENTS = 8
LANES = 128
HALO = 16
MESSAGE = 24


def dot(left, right, left_axis, right_axis):
    return lax.dot_general(
        left,
        right,
        (((left_axis,), (right_axis,)), ((), ())),
        preferred_element_type=jnp.float32,
    )


def flipped(index, bit):
    return index + (1 - 2 * ((index // bit) % 2)) * bit


def kernel(
    n_ctx,
    n_tp,
    length,
    qp_any,
    kp_any,
    vp_any,
    lc_any,
    w_any,
    og_any,
    filt,
    bias,
    residue,
    rate,
    down,
    up,
    q_out,
    k_out,
    v_out,
    down_out,
    up_out,
    qp,
    kp,
    vp,
    lc,
    w,
    og,
    before,
    after,
    ext,
    query,
    key,
    value,
    gated,
    own,
    far_send,
    far_recv,
    x_send,
    x_recv,
    near_send,
    near_recv,
    rank_send,
    rank_recv,
    grad_send,
    grad_recv,
    g,
    qg,
    corr,
    g_lane,
    corr_lane,
    branch,
    decay,
    weight,
    seg,
    full,
    state,
    msg,
    msg_recv,
    load_sem,
    w_sem,
    halo_ss,
    halo_rs,
    far_ss,
    far_rs,
    x_ss,
    x_rs,
    near_ss,
    near_rs,
    rank_ss,
    rank_rs,
    grad_ss,
    grad_rs,
    msg_ss,
    msg_rs,
):
    tokens, channels = qp.shape
    half = channels // 2
    modes = rate.shape[0]
    rank = up.shape[0]
    step = tokens // SEGMENTS
    me = lax.axis_index("ctx")
    tp = lax.axis_index("tp")
    sibling = flipped(tp, 1)
    across = flipped(tp, 2)
    corner = flipped(sibling, 2)

    order = (corner, across, sibling, tp)

    def rows_of(block):
        return pl.ds(pl.multiple_of(block * channels, channels), channels)

    og_load = pltpu.make_async_copy(og_any, og, load_sem.at[0])
    og_load.start()
    w_loads = []
    for i, block in enumerate(order):
        load = pltpu.make_async_copy(w_any.at[rows_of(block)], w.at[i], w_sem.at[i])
        load.start()
        w_loads.append(load)
    loads = []
    for i, (src, dst) in enumerate(((qp_any, qp), (kp_any, kp), (vp_any, vp), (lc_any, lc))):
        load = pltpu.make_async_copy(src, dst, load_sem.at[i + 1])
        load.start()
        loads.append(load)

    barrier = pltpu.get_barrier_semaphore()
    for d in range(1, n_tp):
        pl.semaphore_signal(
            barrier, inc=1, device_id={"tp": lax.rem(tp + d, n_tp)}, device_id_type=MESH
        )
    for d in range(1, n_ctx):
        pl.semaphore_signal(
            barrier, inc=1, device_id={"ctx": lax.rem(me + d, n_ctx)}, device_id_type=MESH
        )

    rates = rate[...] / length
    decay[...] = jnp.exp(-rates)
    weight[...] = residue[...] * jnp.sqrt(rates)

    og_load.wait()
    og_value = og[...]
    low = dot(og_value, up[...], 1, 1)
    low16 = (adapter_scale * low).astype(jnp.bfloat16)
    rank_send[0, :rank] = dot(up[...], og_value, 1, 1)

    def product(i, h):
        columns = pl.ds(
            pl.multiple_of(order[i] * channels + h * half, half), half
        )
        return dot(og_value, w[i, h * half : (h + 1) * half], 1, 1) + dot(
            low16, down[:, columns], 1, 0
        )

    def remote(src, dst, ss, rs, where):
        return pltpu.make_async_remote_copy(
            src_ref=src,
            dst_ref=dst,
            send_sem=ss,
            recv_sem=rs,
            device_id=where,
            device_id_type=MESH,
        )

    w_loads[0].wait()
    far_send[0] = product(0, 0).astype(jnp.bfloat16)
    pl.semaphore_wait(barrier, n_tp + n_ctx - 2)

    far = [
        remote(far_send.at[h], far_recv.at[h], far_ss.at[h], far_rs.at[h], {"tp": sibling})
        for h in range(2)
    ]
    over = [
        remote(x_send.at[h], x_recv.at[h], x_ss.at[h], x_rs.at[h], {"tp": across})
        for h in range(2)
    ]
    near = [
        remote(near_send.at[h], near_recv.at[h], near_ss.at[h], near_rs.at[h], {"tp": sibling})
        for h in range(2)
    ]
    far[0].start()
    far_send[1] = product(0, 1).astype(jnp.bfloat16)
    far[1].start()
    w_loads[1].wait()
    for h in range(2):
        mine = product(1, h)
        far[h].wait_recv()
        x_send[h] = (mine + far_recv[h].astype(jnp.float32)).astype(jnp.bfloat16)
        over[h].start()

    for load in loads:
        load.wait()
    tails = [
        remote(
            src.at[pl.ds(tokens - HALO, HALO)],
            before.at[i],
            halo_ss.at[i],
            halo_rs.at[i],
            {"ctx": lax.rem(me + 1, n_ctx)},
        )
        for i, src in enumerate((qp, kp, vp))
    ]
    heads = [
        remote(
            src.at[pl.ds(0, HALO)],
            after.at[i],
            halo_ss.at[3 + i],
            halo_rs.at[3 + i],
            {"ctx": lax.rem(me + n_ctx - 1, n_ctx)},
        )
        for i, src in enumerate((kp, vp))
    ]

    @pl.when(me < n_ctx - 1)
    def _():
        for copy in tails:
            copy.start()

    @pl.when(me > 0)
    def _():
        for copy in heads:
            copy.start()

    w_loads[2].wait()
    for h in range(2):
        near_send[h] = product(2, h).astype(jnp.bfloat16)
        near[h].start()
    w_loads[3].wait()
    for h in range(2):
        own[:, h * half : (h + 1) * half] = product(3, h)

    @pl.when(me > 0)
    def _():
        for copy in tails:
            copy.wait_recv()

    @pl.when(me == 0)
    def _():
        before[...] = jnp.zeros_like(before)

    @pl.when(me < n_ctx - 1)
    def _():
        for copy in heads:
            copy.wait_recv()

    @pl.when(me == n_ctx - 1)
    def _():
        after[...] = jnp.zeros_like(after)

    def short_conv(index, src, dst, rows):
        ext[0:8] = before[index].astype(jnp.float32)[HALO - 8 :]
        ext[8 : 8 + tokens] = src[...].astype(jnp.float32)
        if index > 0:
            ext[8 + tokens : 16 + tokens] = after[index - 1].astype(jnp.float32)[:8]
        dst[0:rows] = (
            filt[index, 0:1] * ext[8 : 8 + rows]
            + filt[index, 1:2] * ext[7 : 7 + rows]
            + filt[index, 2:3] * ext[6 : 6 + rows]
        )

    short_conv(0, qp, query, tokens)
    gated[...] = (query[...] * lc[...].astype(jnp.float32)).astype(jnp.bfloat16)
    rank_send[0, rank:] = dot(down[:, rows_of(tp)], gated[...], 1, 1)

    rank_rounds = [
        remote(
            rank_send.at[k],
            rank_recv.at[k],
            rank_ss.at[k],
            rank_rs.at[k],
            {"tp": flipped(tp, 1 << k)},
        )
        for k in range(n_tp.bit_length() - 1)
    ]
    grad_rounds = [
        remote(
            grad_send.at[k],
            grad_recv.at[k],
            grad_ss.at[k],
            grad_rs.at[k],
            {"ctx": flipped(me, 1 << k)},
        )
        for k in range(n_ctx.bit_length() - 1)
    ]
    rank_rounds[0].start()
    short_conv(1, kp, key, tokens + 8)
    rank_rounds[0].wait_recv()
    rank_send[1] = rank_send[0] + rank_recv[0]
    rank_rounds[1].start()
    short_conv(2, vp, value, tokens + 8)

    msgs = []
    for h in range(2):
        near[h].wait_recv()
        over[h].wait_recv()
        lanes = slice(h * half, (h + 1) * half)
        gate = (
            own[:, lanes]
            + near_recv[h].astype(jnp.float32)
            + x_recv[h].astype(jnp.float32)
        )
        qg[0:tokens, lanes] = gate * lc[:, lanes].astype(jnp.float32)
        g[0:tokens, lanes] = gate * query[:, lanes]
        groups = range(h * half // LANES, (h + 1) * half // LANES)
        for group in groups:
            g_lane[group] = g[0:tokens, group * LANES : (group + 1) * LANES]
        for lane in range(h * half, (h + 1) * half, LANES):
            cols = pl.ds(lane, LANES)
            decays = [
                jnp.broadcast_to(decay[n : n + 1, cols], (SEGMENTS, LANES)) for n in range(modes)
            ]

            def back(i, held, group=lane // LANES, decays=decays):
                row = g_lane[group, pl.ds(step - 1 - i, SEGMENTS, stride=step), :]
                return tuple(a * x + row for a, x in zip(decays, held))

            zero = jnp.zeros((SEGMENTS, LANES), jnp.float32)
            held = lax.fori_loop(0, step - 1, back, (zero,) * modes, unroll=True)
            for n in range(modes):
                seg[lane // LANES, pl.ds(n, SEGMENTS, stride=modes), :] = held[n]
        a = decay[:, lanes]
        rest = jnp.exp(-rates[:, lanes] * (step - 1))
        ahead = jnp.zeros((modes, half), jnp.float32)
        for s in range(SEGMENTS - 1, -1, -1):
            local = [seg[group, s * modes : (s + 1) * modes] for group in groups]
            second = jnp.concatenate(local, axis=1) + rest * ahead
            ahead = a * second + g[s * step : s * step + 1, lanes]
            full[s * modes : (s + 1) * modes, lanes] = ahead
        msg[h, 0:modes] = second
        msg[h, modes : modes + 2] = g[0:2, lanes]
        msg[h, modes + 2 : modes + 4] = qg[0:2, lanes]
        msg[h, modes + 4 :] = jnp.zeros((MESSAGE - modes - 4, half), jnp.float32)
        for d in range(1, n_ctx):
            copy = remote(
                msg.at[h],
                msg_recv.at[d - 1, h],
                msg_ss.at[d - 1, h],
                msg_rs.at[d - 1, h],
                {"ctx": lax.rem(me + n_ctx - d, n_ctx)},
            )
            msgs.append((d, h, copy))

            @pl.when(me >= d)
            def _(copy=copy):
                copy.start()

    rank_rounds[1].wait_recv()
    sums = (rank_send[1] + rank_recv[1]).astype(jnp.bfloat16)
    grad_send[0, :rank] = dot(sums[:rank], gated[...], 1, 0)
    grad_send[0, rank:] = dot(sums[rank:], og_value, 1, 0)
    grad_rounds[0].start()

    def out_rows(index, src, dst, first, last):
        dst[first:last] = (
            filt[index, 0:1] * src[first:last]
            + filt[index, 1:2] * src[first + 1 : last + 1]
            + filt[index, 2:3] * src[first + 2 : last + 2]
        ).astype(jnp.bfloat16)

    out_rows(0, qg, q_out, 0, tokens - HALO)
    g[tokens:] = jnp.zeros((8, channels), jnp.float32)
    qg[tokens:] = jnp.zeros((8, channels), jnp.float32)
    corr[tokens:] = jnp.zeros((8, channels), jnp.float32)
    state[...] = jnp.zeros_like(state)
    for h in range(2):
        lanes = slice(h * half, (h + 1) * half)
        a = decay[:, lanes]
        for d, at, copy in msgs:
            if at != h:
                continue

            @pl.when(me + d < n_ctx)
            def _(d=d, copy=copy, lanes=lanes, a=a, h=h):
                copy.wait_recv()
                got = msg_recv[d - 1, h]
                if d == 1:
                    state[:, lanes] = got[:modes]
                    g[tokens : tokens + 2, lanes] = got[modes : modes + 2]
                    qg[tokens : tokens + 2, lanes] = got[modes + 2 : modes + 4]
                else:
                    gone = jnp.exp(-rates[:, lanes] * (tokens * (d - 1) - 1))
                    state[:, lanes] += gone * (a * got[:modes] + got[modes : modes + 1])

        second = state[:, lanes]
        first = a * second + g[tokens : tokens + 1, lanes]
        corr[tokens : tokens + 1, lanes] = jnp.sum(
            weight[:, lanes] * first, axis=0, keepdims=True
        )
        corr[tokens + 1 : tokens + 2, lanes] = jnp.sum(
            weight[:, lanes] * second, axis=0, keepdims=True
        )
        whole = jnp.exp(-rates[:, lanes] * step)
        carry = first
        for s in range(SEGMENTS - 1, -1, -1):
            at = slice(s * modes, (s + 1) * modes)
            for j in range(half // LANES):
                seg[h * half // LANES + j, at] = carry[:, j * LANES : (j + 1) * LANES]
            if s > 0:
                own_state = full[at, lanes]
                first = whole * first
                carry = own_state + first

        for lane in range(h * half, (h + 1) * half, LANES):
            cols = pl.ds(lane, LANES)
            decays = [
                jnp.broadcast_to(decay[n : n + 1, cols], (SEGMENTS, LANES)) for n in range(modes)
            ]
            weights = [
                jnp.broadcast_to(weight[n : n + 1, cols], (SEGMENTS, LANES)) for n in range(modes)
            ]

            def back(i, held, group=lane // LANES, decays=decays, weights=weights):
                at = pl.ds(step - 1 - i, SEGMENTS, stride=step)
                row = g_lane[group, at, :]
                held = tuple(a * x + row for a, x in zip(decays, held))
                terms = [b * x for b, x in zip(weights, held)]
                while len(terms) > 1:
                    terms = [
                        terms[j] + terms[j + 1] if j + 1 < len(terms) else terms[j]
                        for j in range(0, len(terms), 2)
                    ]
                corr_lane[group, at, :] = terms[0]
                return held

            start = tuple(
                seg[lane // LANES, pl.ds(n, SEGMENTS, stride=modes), :] for n in range(modes)
            )
            lax.fori_loop(0, step, back, start, unroll=True)
            corr[0:tokens, lane : lane + LANES] = corr_lane[lane // LANES]

    grad_now = grad_send[0]
    for k, copy in enumerate(grad_rounds):
        copy.wait_recv()
        grad_now = grad_now + grad_recv[k]
        if k + 1 < len(grad_rounds):
            grad_send[k + 1] = grad_now
            grad_rounds[k + 1].start()

    out_rows(0, qg, q_out, tokens - HALO, tokens)
    corr[...] = corr[...] + bias[...] * g[...]
    branch[...] = corr[...] * value[...]
    out_rows(1, branch, k_out, 0, tokens)
    branch[...] = corr[...] * key[...]
    out_rows(2, branch, v_out, 0, tokens)
    scale = adapter_scale / math.sqrt(length)
    down_out[...] = grad_now[:rank] * scale
    up_out[...] = grad_now[rank:] * scale

    for copy in far + over + near + rank_rounds + grad_rounds:
        copy.wait_send()

    @pl.when(me < n_ctx - 1)
    def _():
        for copy in tails:
            copy.wait_send()

    @pl.when(me > 0)
    def _():
        for copy in heads:
            copy.wait_send()

    for d, h, copy in msgs:

        @pl.when(me >= d)
        def _(copy=copy):
            copy.wait_send()


def on_device(
    n_ctx,
    n_tp,
    query_projected,
    key_projected,
    value_projected,
    long_conv_output,
    short_conv_filter,
    direct_bias,
    mode_residue,
    mode_decay_rate,
    output_weight,
    adapter_down_factor,
    adapter_up_factor,
    output_gradient,
):
    tokens, channels = query_projected.shape
    features = output_gradient.shape[1]
    modes = mode_residue.shape[1]
    rank = adapter_up_factor.shape[0]
    half = channels // 2
    f32, bf16 = jnp.float32, jnp.bfloat16
    rank_rounds = n_tp.bit_length() - 1
    grad_rounds = n_ctx.bit_length() - 1
    vmem = pl.BlockSpec(memory_space=pltpu.VMEM)
    anywhere = pl.BlockSpec(memory_space=pl.ANY)
    buffer = pltpu.VMEM
    dma = pltpu.SemaphoreType.DMA
    pair = (2, tokens, half)
    outs = pl.pallas_call(
        functools.partial(kernel, n_ctx, n_tp, tokens * n_ctx),
        out_shape=(
            jax.ShapeDtypeStruct((tokens, channels), bf16),
            jax.ShapeDtypeStruct((tokens, channels), bf16),
            jax.ShapeDtypeStruct((tokens, channels), bf16),
            jax.ShapeDtypeStruct((rank, channels), f32),
            jax.ShapeDtypeStruct((rank, features), f32),
        ),
        in_specs=[anywhere] * 6 + [vmem] * 6,
        out_specs=(vmem,) * 5,
        scratch_shapes=[
            buffer((tokens, channels), bf16),
            buffer((tokens, channels), bf16),
            buffer((tokens, channels), bf16),
            buffer((tokens, channels), bf16),
            buffer((n_tp, channels, features), bf16),
            buffer((tokens, features), bf16),
            buffer((3, HALO, channels), bf16),
            buffer((2, HALO, channels), bf16),
            buffer((tokens + 16, channels), f32),
            buffer((tokens, channels), f32),
            buffer((tokens + 8, channels), f32),
            buffer((tokens + 8, channels), f32),
            buffer((tokens, channels), bf16),
            buffer((tokens, channels), f32),
            buffer(pair, bf16),
            buffer(pair, bf16),
            buffer(pair, bf16),
            buffer(pair, bf16),
            buffer(pair, bf16),
            buffer(pair, bf16),
            buffer((rank_rounds, 2 * rank, tokens), f32),
            buffer((rank_rounds, 2 * rank, tokens), f32),
            buffer((grad_rounds, 2 * rank, channels), f32),
            buffer((grad_rounds, 2 * rank, channels), f32),
            buffer((tokens + 8, channels), f32),
            buffer((tokens + 8, channels), f32),
            buffer((tokens + 8, channels), f32),
            buffer((channels // LANES, tokens, LANES), f32),
            buffer((channels // LANES, tokens, LANES), f32),
            buffer((tokens + 8, channels), f32),
            buffer((modes, channels), f32),
            buffer((modes, channels), f32),
            buffer((channels // LANES, SEGMENTS * modes, LANES), f32),
            buffer((SEGMENTS * modes, channels), f32),
            buffer((modes, channels), f32),
            buffer((2, MESSAGE, half), f32),
            buffer((n_ctx - 1, 2, MESSAGE, half), f32),
            dma((5,)),
            dma((n_tp,)),
            dma((5,)),
            dma((5,)),
            dma((2,)),
            dma((2,)),
            dma((2,)),
            dma((2,)),
            dma((2,)),
            dma((2,)),
            dma((rank_rounds,)),
            dma((rank_rounds,)),
            dma((grad_rounds,)),
            dma((grad_rounds,)),
            dma((n_ctx - 1, 2)),
            dma((n_ctx - 1, 2)),
        ],
        compiler_params=pltpu.CompilerParams(
            collective_id=0, has_side_effects=True, vmem_limit_bytes=40 * 1024 * 1024
        ),
    )(
        query_projected,
        key_projected,
        value_projected,
        long_conv_output,
        output_weight,
        output_gradient,
        short_conv_filter,
        direct_bias.reshape(1, channels),
        mode_residue.T,
        mode_decay_rate.T,
        adapter_down_factor.T,
        adapter_up_factor,
    )
    return (outs[0], outs[1], outs[2], outs[3].T, outs[4])


def solution(mesh):
    in_specs = (
        P(("grp", "ctx"), "tp"),
        P(("grp", "ctx"), "tp"),
        P(("grp", "ctx"), "tp"),
        P(("grp", "ctx"), "tp"),
        P(None, None, "tp"),
        P("tp"),
        P("tp", None),
        P("tp", None),
        P(None, "tp"),
        P(),
        P(None, "tp"),
        P(("grp", "ctx"), "tp"),
    )
    out_specs = (
        P(("grp", "ctx"), "tp"),
        P(("grp", "ctx"), "tp"),
        P(("grp", "ctx"), "tp"),
        P(("grp", "tp"), None),
        P("grp", "tp"),
    )
    return jax.shard_map(
        functools.partial(on_device, mesh.shape["ctx"], mesh.shape["tp"]),
        mesh=mesh,
        in_specs=in_specs,
        out_specs=out_specs,
        check_vma=False,
    )
```

time: 163 us -> 39.5 us (0.24)
  waiting for transfers between devices: 51.4 us -> 0 us
  matrix products: 36.2 us -> 0 us
  Pallas kernels: 0 us -> 24.2 us
  other arithmetic: 19.7 us -> 0 us
  starting transfers between devices: 15.5 us -> 0 us
  between operations: 16.1 us -> 0.67 us
  blocking collectives: 11.4 us -> 0 us
  local copies, waits for them, and re-layouts: 11.4 us -> 14 us
    psum x2 -> x0, waiting for transfers between devices: 42.9 us -> none  [the longest x1 34.4 us: on_device(): down_factor_sum, up_factor_sum = lax.psum((down_part, up_part), 'ctx')]
    dot_general x24 -> x0, matrix products: 36.2 us -> none  [the longest x3 4 us: contract_final_axis(): lax.dot_general(left, right, (((1,), (1,)), ((), ())), preferred_element_...]
    pallas_call x0 -> x1, Pallas kernels: none -> 24.2 us  [on_device(): pl.pallas_call(functools.partial(kernel, n_ctx, n_tp, tokens * n_ctx), ou...]
    psum x1 -> x0, blocking collectives: 11.4 us -> none  [on_device(): adapter_sum, act_sum = lax.psum((adapter_portion, act_part), 'tp')]
    unnamed x53 -> x29, local copies, waits for them, and re-layouts: 3.48 us -> 14 us
    all_to_all x2 -> x0, starting transfers between devices: 8.6 us -> none  [the longest x1 4.6 us: on_device(): lax.all_to_all(outgoing.astype(jnp.bfloat16), 'ctx', split_axis=0, concat...]
    convert_element_type x24 -> x0, other arithmetic: 8.16 us -> none  [the longest x1 1.73 us: on_device(): value_projected.astype(jnp.float32)]
    ppermute x2 -> x0, starting transfers between devices: 6.8 us -> none  [passed_along(): return lax.ppermute(value, axis, pairs)]
  transfers between devices with their start and end apart: 6 -> 0, of which waited for: 4 -> 0; matrix products, arithmetic and copies ran while one was open for 15% -> 0% of each run, Pallas kernels for 0% -> 0%
where the time goes in v1:
time: 39.5 us; the launch traced here: 38.9 us
  Pallas kernels  24.2 us (61%)
  local copies, waits for them, and re-layouts  14 us (35%)
  between operations  0.67 us (2%)
    pallas_call x1, Pallas kernels, on_device(): pl.pallas_call(functools.partial(kernel, n_ctx, n_tp, tokens * n_ctx), ou...  24.2 us
    unnamed x29, local copies, waits for them, and re-layouts  14 us

profile of v1, /device:TPU:0, one launch (start us, length us, event | category | flops | bytes accessed | tf_op | source)
XLA Modules:
  0.0 38.9 jit_solution(17928744220947765478)
XLA Ops:
  0.6 0.0 copy-start
  0.6 1.6 %copy-done = bf16[2048,512]{1,0:T(8,128)(2,1)S(1)} copy-done((bf16[2048,512]{1,0:T(8,128)(2,1)S(1)}, bf16[2048,512]{1,0:T(8,128)(2,1)}, u32[]{:S(2)}) %copy-start) | copy-done | bytes 2097176
  2.2 0.0 copy-start.1
  2.2 0.9 %copy-done.1 = bf16[192,512]{1,0:T(8,128)(2,1)S(1)} copy-done((bf16[192,512]{1,0:T(8,128)(2,1)S(1)}, bf16[192,512]{1,0:T(8,128)(2,1)}, u32[]{:S(2)}) %copy-start.1) | copy-done | bytes 196632
  3.2 0.0 copy-start.2
  3.2 0.9 %copy-done.2 = bf16[192,512]{1,0:T(8,128)(2,1)S(1)} copy-done((bf16[192,512]{1,0:T(8,128)(2,1)S(1)}, bf16[192,512]{1,0:T(8,128)(2,1)}, u32[]{:S(2)}) %copy-start.2) | copy-done | bytes 196632
  4.1 0.0 copy-start.3
  4.1 0.9 %copy-done.3 = bf16[192,512]{1,0:T(8,128)(2,1)S(1)} copy-done((bf16[192,512]{1,0:T(8,128)(2,1)S(1)}, bf16[192,512]{1,0:T(8,128)(2,1)}, u32[]{:S(2)}) %copy-start.3) | copy-done | bytes 196632
  5.0 0.0 copy-start.4
  5.0 0.9 %copy-done.4 = bf16[192,512]{1,0:T(8,128)(2,1)S(1)} copy-done((bf16[192,512]{1,0:T(8,128)(2,1)S(1)}, bf16[192,512]{1,0:T(8,128)(2,1)}, u32[]{:S(2)}) %copy-start.4) | copy-done | bytes 196632
  5.9 0.0 copy-start.5
  5.9 0.9 %copy-done.5 = bf16[192,512]{1,0:T(8,128)(2,1)S(1)} copy-done((bf16[192,512]{1,0:T(8,128)(2,1)S(1)}, bf16[192,512]{1,0:T(8,128)(2,1)}, u32[]{:S(2)}) %copy-start.5) | copy-done | bytes 196632
  6.9 0.0 copy-start.6
  6.9 0.8 %copy-done.6 = bf16[2048,16]{0,1:T(8,128)(2,1)S(1)} copy-done((bf16[2048,16]{0,1:T(8,128)(2,1)S(1)}, bf16[2048,16]{0,1:T(8,128)(2,1)}, u32[]{:S(2)}) %copy-start.6) | copy-done | bytes 65560
  7.7 0.0 copy-start.7
  7.7 0.8 %copy-done.7 = f32[512,16]{0,1:T(8,128)S(1)} copy-done((f32[512,16]{0,1:T(8,128)S(1)}, f32[512,16]{0,1:T(8,128)}, u32[]{:S(2)}) %copy-start.7) | copy-done | bytes 32792
  8.5 0.0 copy-start.8
  8.5 0.8 %copy-done.8 = f32[512,16]{0,1:T(8,128)S(1)} copy-done((f32[512,16]{0,1:T(8,128)S(1)}, f32[512,16]{0,1:T(8,128)}, u32[]{:S(2)}) %copy-start.8) | copy-done | bytes 32792
  9.2 0.0 copy-start.9
  9.2 0.7 %copy-done.9 = f32[3,3,512]{2,1,0:T(4,128)S(1)} copy-done((f32[3,3,512]{2,1,0:T(4,128)S(1)}, f32[3,3,512]{2,1,0:T(4,128)}, u32[]{:S(2)}) %copy-start.9) | copy-done | bytes 18456
  10.0 0.0 copy-start.10
  10.0 0.7 %copy-done.10 = bf16[16,512]{1,0:T(8,128)(2,1)S(1)} copy-done((bf16[16,512]{1,0:T(8,128)(2,1)S(1)}, bf16[16,512]{1,0:T(8,128)(2,1)}, u32[]{:S(2)}) %copy-start.10) | copy-done | bytes 16408
  10.7 0.0 copy-start.11
  10.7 0.7 %copy-done.11 = f32[512]{0:T(512)S(1)} copy-done((f32[512]{0:T(512)S(1)}, f32[512]{0:T(512)}, u32[]{:S(2)}) %copy-start.11) | copy-done | bytes 2072
  11.4 24.2 %shard_map.155 = (bf16[192,512]{1,0:T(8,128)(2,1)S(1)}, bf16[192,512]{1,0:T(8,128)(2,1)S(1)}, bf16[192,512]{1,0:T(8,128)(2,1)S(1)}, f32[16,512]{1,0:T(8,128)S(1)}, f32[16,512]{1,0:T(8,128)S(1)}) custom-call(bf16[192,512]{1,0:T(8,128)(2,1)S(1)} %copy-done.1, bf16[192,512]{1,0:T(8,128)(2,1)S(1)} %copy-done.2, bf16[192,512]{1,0:T(8,128)(2,1)S(1)} %copy-done.3, ...), custom_call_target="tpu_custom_call" | custom-call | tf_op jit(solution)/shard_map/pallas_call | solution.py:507
  35.6 0.7 %copy.22 = bf16[192,512]{1,0:T(8,128)(2,1)} copy(bf16[192,512]{1,0:T(8,128)(2,1)S(1)} %get-tuple-element.20) | data formatting | bytes 393216
  36.3 0.7 %copy.23 = bf16[192,512]{1,0:T(8,128)(2,1)} copy(bf16[192,512]{1,0:T(8,128)(2,1)S(1)} %get-tuple-element.21) | data formatting | bytes 393216
  37.0 0.7 %copy.24 = bf16[192,512]{1,0:T(8,128)(2,1)} copy(bf16[192,512]{1,0:T(8,128)(2,1)S(1)} %get-tuple-element.22) | data formatting | bytes 393216
  37.6 0.6 %copy.25 = f32[512,16]{0,1:T(8,128)} copy(f32[512,16]{0,1:T(8,128)S(1)} %bitcast.8) | data formatting | bytes 65536
  38.3 0.6 %copy.26 = f32[16,512]{1,0:T(8,128)} copy(f32[16,512]{1,0:T(8,128)S(1)} %get-tuple-element.24) | data formatting | bytes 65536
Async XLA Ops:
  0.6 1.6 %copy-start = (bf16[2048,512]{1,0:T(8,128)(2,1)S(1)}, bf16[2048,512]{1,0:T(8,128)(2,1)}, u32[]{:S(2)}) copy-start(bf16[2048,512]{1,0:T(8,128)(2,1)} %w_any.1) | copy-start | bytes 6291460
  2.2 0.9 %copy-start.1 = (bf16[192,512]{1,0:T(8,128)(2,1)S(1)}, bf16[192,512]{1,0:T(8,128)(2,1)}, u32[]{:S(2)}) copy-start(bf16[192,512]{1,0:T(8,128)(2,1)} %qp_any.1) | copy-start | bytes 589828
  3.2 0.9 %copy-start.2 = (bf16[192,512]{1,0:T(8,128)(2,1)S(1)}, bf16[192,512]{1,0:T(8,128)(2,1)}, u32[]{:S(2)}) copy-start(bf16[192,512]{1,0:T(8,128)(2,1)} %kp_any.1) | copy-start | bytes 589828
  4.1 0.9 %copy-start.3 = (bf16[192,512]{1,0:T(8,128)(2,1)S(1)}, bf16[192,512]{1,0:T(8,128)(2,1)}, u32[]{:S(2)}) copy-start(bf16[192,512]{1,0:T(8,128)(2,1)} %vp_any.1) | copy-start | bytes 589828
  5.0 0.9 %copy-start.4 = (bf16[192,512]{1,0:T(8,128)(2,1)S(1)}, bf16[192,512]{1,0:T(8,128)(2,1)}, u32[]{:S(2)}) copy-start(bf16[192,512]{1,0:T(8,128)(2,1)} %lc_any.1) | copy-start | bytes 589828
  5.9 0.9 %copy-start.5 = (bf16[192,512]{1,0:T(8,128)(2,1)S(1)}, bf16[192,512]{1,0:T(8,128)(2,1)}, u32[]{:S(2)}) copy-start(bf16[192,512]{1,0:T(8,128)(2,1)} %og_any.1) | copy-start | bytes 589828
  6.9 0.8 %copy-start.6 = (bf16[2048,16]{0,1:T(8,128)(2,1)S(1)}, bf16[2048,16]{0,1:T(8,128)(2,1)}, u32[]{:S(2)}) copy-start(bf16[2048,16]{0,1:T(8,128)(2,1)} %param.21) | copy-start | bytes 196612
  7.7 0.8 %copy-start.7 = (f32[512,16]{0,1:T(8,128)S(1)}, f32[512,16]{0,1:T(8,128)}, u32[]{:S(2)}) copy-start(f32[512,16]{0,1:T(8,128)} %param.18) | copy-start | bytes 98308
  8.5 0.8 %copy-start.8 = (f32[512,16]{0,1:T(8,128)S(1)}, f32[512,16]{0,1:T(8,128)}, u32[]{:S(2)}) copy-start(f32[512,16]{0,1:T(8,128)} %param.19) | copy-start | bytes 98308
  9.2 0.7 %copy-start.9 = (f32[3,3,512]{2,1,0:T(4,128)S(1)}, f32[3,3,512]{2,1,0:T(4,128)}, u32[]{:S(2)}) copy-start(f32[3,3,512]{2,1,0:T(4,128)} %filt.1) | copy-start | bytes 55300
  10.0 0.7 %copy-start.10 = (bf16[16,512]{1,0:T(8,128)(2,1)S(1)}, bf16[16,512]{1,0:T(8,128)(2,1)}, u32[]{:S(2)}) copy-start(bf16[16,512]{1,0:T(8,128)(2,1)} %up.1) | copy-start | bytes 49156
  10.7 0.7 %copy-start.11 = (f32[512]{0:T(512)S(1)}, f32[512]{0:T(512)}, u32[]{:S(2)}) copy-start(f32[512]{0:T(512)} %param.17) | copy-start | bytes 6148

commit v2 on v1

--- a/solution.py
+++ b/solution.py
@@ -13,7 +13,6 @@
 SEGMENTS = 8
 LANES = 128
 HALO = 16
-MESSAGE = 24
 
 
 def dot(left, right, left_axis, right_axis):
@@ -39,12 +38,12 @@
     lc_any,
     w_any,
     og_any,
-    filt,
-    bias,
-    residue,
-    rate,
-    down,
-    up,
+    filt_any,
+    bias_any,
+    residue_any,
+    rate_any,
+    down_any,
+    up_any,
     q_out,
     k_out,
     v_out,
@@ -56,6 +55,12 @@
     lc,
     w,
     og,
+    filt,
+    bias,
+    residue,
+    rate,
+    down,
+    up,
     before,
     after,
     ext,
@@ -87,6 +92,8 @@
     state,
     msg,
     msg_recv,
+    far_msg,
+    far_msg_recv,
     load_sem,
     w_sem,
     halo_ss,
@@ -115,39 +122,50 @@
     across = flipped(tp, 2)
     corner = flipped(sibling, 2)
 
+    barrier = pltpu.get_barrier_semaphore()
+    for d in range(1, n_tp):
+        pl.semaphore_signal(
+            barrier, inc=1, device_id={"tp": lax.rem(tp + d, n_tp)}, device_id_type=MESH
+        )
+    for d in range(1, n_ctx):
+        pl.semaphore_signal(
+            barrier, inc=1, device_id={"ctx": lax.rem(me + d, n_ctx)}, device_id_type=MESH
+        )
+
     order = (corner, across, sibling, tp)
 
     def rows_of(block):
         return pl.ds(pl.multiple_of(block * channels, channels), channels)
 
-    og_load = pltpu.make_async_copy(og_any, og, load_sem.at[0])
-    og_load.start()
+    first_loads = []
+    for i, (src, dst) in enumerate(((og_any, og), (up_any, up), (down_any, down))):
+        load = pltpu.make_async_copy(src, dst, load_sem.at[i])
+        load.start()
+        first_loads.append(load)
     w_loads = []
     for i, block in enumerate(order):
         load = pltpu.make_async_copy(w_any.at[rows_of(block)], w.at[i], w_sem.at[i])
         load.start()
         w_loads.append(load)
     loads = []
-    for i, (src, dst) in enumerate(((qp_any, qp), (kp_any, kp), (vp_any, vp), (lc_any, lc))):
-        load = pltpu.make_async_copy(src, dst, load_sem.at[i + 1])
+    for i, (src, dst) in enumerate(
+        (
+            (rate_any, rate),
+            (residue_any, residue),
+            (qp_any, qp),
+            (kp_any, kp),
+            (vp_any, vp),
+            (lc_any, lc),
+            (filt_any, filt),
+            (bias_any, bias),
+        )
+    ):
+        load = pltpu.make_async_copy(src, dst, load_sem.at[i + 3])
         load.start()
         loads.append(load)
 
-    barrier = pltpu.get_barrier_semaphore()
-    for d in range(1, n_tp):
-        pl.semaphore_signal(
-            barrier, inc=1, device_id={"tp": lax.rem(tp + d, n_tp)}, device_id_type=MESH
-        )
-    for d in range(1, n_ctx):
-        pl.semaphore_signal(
-            barrier, inc=1, device_id={"ctx": lax.rem(me + d, n_ctx)}, device_id_type=MESH
-        )
-
-    rates = rate[...] / length
-    decay[...] = jnp.exp(-rates)
-    weight[...] = residue[...] * jnp.sqrt(rates)
-
-    og_load.wait()
+    for load in first_loads:
+        load.wait()
     og_value = og[...]
     low = dot(og_value, up[...], 1, 1)
     low16 = (adapter_scale * low).astype(jnp.bfloat16)
@@ -170,10 +188,6 @@
             device_id=where,
             device_id_type=MESH,
         )
-
-    w_loads[0].wait()
-    far_send[0] = product(0, 0).astype(jnp.bfloat16)
-    pl.semaphore_wait(barrier, n_tp + n_ctx - 2)
 
     far = [
         remote(far_send.at[h], far_recv.at[h], far_ss.at[h], far_rs.at[h], {"tp": sibling})
@@ -187,18 +201,6 @@
         remote(near_send.at[h], near_recv.at[h], near_ss.at[h], near_rs.at[h], {"tp": sibling})
         for h in range(2)
     ]
-    far[0].start()
-    far_send[1] = product(0, 1).astype(jnp.bfloat16)
-    far[1].start()
-    w_loads[1].wait()
-    for h in range(2):
-        mine = product(1, h)
-        far[h].wait_recv()
-        x_send[h] = (mine + far_recv[h].astype(jnp.float32)).astype(jnp.bfloat16)
-        over[h].start()
-
-    for load in loads:
-        load.wait()
     tails = [
         remote(
             src.at[pl.ds(tokens - HALO, HALO)],
@@ -220,6 +222,16 @@
         for i, src in enumerate((kp, vp))
     ]
 
+    for load in loads:
+        load.wait()
+    w_loads[0].wait()
+    w_loads[1].wait()
+    for h in range(2):
+        far_send[h] = product(0, h).astype(jnp.bfloat16)
+    pl.semaphore_wait(barrier, n_tp + n_ctx - 2)
+    for h in range(2):
+        far[h].start()
+
     @pl.when(me < n_ctx - 1)
     def _():
         for copy in tails:
@@ -230,14 +242,24 @@
         for copy in heads:
             copy.start()
 
-    w_loads[2].wait()
+    for h in range(2):
+        own[:, h * half : (h + 1) * half] = product(1, h)
+
+    for i in range(2):
+        w_loads[2 + i].wait()
     for h in range(2):
         near_send[h] = product(2, h).astype(jnp.bfloat16)
         near[h].start()
-    w_loads[3].wait()
+    for h in range(2):
+        far[h].wait_recv()
+        lanes = slice(h * half, (h + 1) * half)
+        x_send[h] = (own[:, lanes] + far_recv[h].astype(jnp.float32)).astype(jnp.bfloat16)
+        over[h].start()
     for h in range(2):
         own[:, h * half : (h + 1) * half] = product(3, h)
-
+    rates = rate[...] / length
+    decay[...] = jnp.exp(-rates)
+    weight[...] = residue[...] * jnp.sqrt(rates)
     @pl.when(me > 0)
     def _():
         for copy in tails:
@@ -293,10 +315,25 @@
     ]
     rank_rounds[0].start()
     short_conv(1, kp, key, tokens + 8)
+    short_conv(2, vp, value, tokens + 8)
     rank_rounds[0].wait_recv()
     rank_send[1] = rank_send[0] + rank_recv[0]
     rank_rounds[1].start()
-    short_conv(2, vp, value, tokens + 8)
+
+    def adapter_gradients():
+        rank_rounds[1].wait_recv()
+        sums = (rank_send[1] + rank_recv[1]).astype(jnp.bfloat16)
+        grad_send[0, :rank] = dot(sums[:rank], gated[...], 1, 0).astype(jnp.bfloat16)
+        grad_send[0, rank:] = dot(sums[rank:], og_value, 1, 0).astype(jnp.bfloat16)
+        grad_rounds[0].start()
+
+    def next_grad_round(k):
+        grad_rounds[k].wait_recv()
+        total = grad_send[k].astype(jnp.float32) + grad_recv[k].astype(jnp.float32)
+        if k + 1 < len(grad_rounds):
+            grad_send[k + 1] = total.astype(jnp.bfloat16)
+            grad_rounds[k + 1].start()
+        return total
 
     msgs = []
     for h in range(2):
@@ -335,14 +372,16 @@
             second = jnp.concatenate(local, axis=1) + rest * ahead
             ahead = a * second + g[s * step : s * step + 1, lanes]
             full[s * modes : (s + 1) * modes, lanes] = ahead
-        msg[h, 0:modes] = second
-        msg[h, modes : modes + 2] = g[0:2, lanes]
-        msg[h, modes + 2 : modes + 4] = qg[0:2, lanes]
-        msg[h, modes + 4 :] = jnp.zeros((MESSAGE - modes - 4, half), jnp.float32)
+        msg[h, 0:modes] = second.astype(jnp.bfloat16)
+        edges = jnp.concatenate(
+            [g[0:2, lanes], qg[0:2, lanes], jnp.zeros((modes - 4, half), jnp.float32)], axis=0
+        )
+        msg[h, modes:] = edges.astype(jnp.bfloat16)
+        far_msg[h] = ahead.astype(jnp.bfloat16)
         for d in range(1, n_ctx):
             copy = remote(
-                msg.at[h],
-                msg_recv.at[d - 1, h],
+                msg.at[h] if d == 1 else far_msg.at[h],
+                msg_recv.at[h] if d == 1 else far_msg_recv.at[d - 2, h],
                 msg_ss.at[d - 1, h],
                 msg_rs.at[d - 1, h],
                 {"ctx": lax.rem(me + n_ctx - d, n_ctx)},
@@ -353,11 +392,8 @@
             def _(copy=copy):
                 copy.start()
 
-    rank_rounds[1].wait_recv()
-    sums = (rank_send[1] + rank_recv[1]).astype(jnp.bfloat16)
-    grad_send[0, :rank] = dot(sums[:rank], gated[...], 1, 0)
-    grad_send[0, rank:] = dot(sums[rank:], og_value, 1, 0)
-    grad_rounds[0].start()
+        if h == 0:
+            adapter_gradients()
 
     def out_rows(index, src, dst, first, last):
         dst[first:last] = (
@@ -367,6 +403,8 @@
         ).astype(jnp.bfloat16)
 
     out_rows(0, qg, q_out, 0, tokens - HALO)
+    for k in range(len(grad_rounds) - 1):
+        next_grad_round(k)
     g[tokens:] = jnp.zeros((8, channels), jnp.float32)
     qg[tokens:] = jnp.zeros((8, channels), jnp.float32)
     corr[tokens:] = jnp.zeros((8, channels), jnp.float32)
@@ -379,16 +417,16 @@
                 continue
 
             @pl.when(me + d < n_ctx)
-            def _(d=d, copy=copy, lanes=lanes, a=a, h=h):
+            def _(d=d, copy=copy, lanes=lanes, h=h):
                 copy.wait_recv()
-                got = msg_recv[d - 1, h]
                 if d == 1:
+                    got = msg_recv[h].astype(jnp.float32)
                     state[:, lanes] = got[:modes]
                     g[tokens : tokens + 2, lanes] = got[modes : modes + 2]
                     qg[tokens : tokens + 2, lanes] = got[modes + 2 : modes + 4]
                 else:
                     gone = jnp.exp(-rates[:, lanes] * (tokens * (d - 1) - 1))
-                    state[:, lanes] += gone * (a * got[:modes] + got[modes : modes + 1])
+                    state[:, lanes] += gone * far_msg_recv[d - 2, h].astype(jnp.float32)
 
         second = state[:, lanes]
         first = a * second + g[tokens : tokens + 1, lanes]
@@ -437,20 +475,13 @@
             lax.fori_loop(0, step, back, start, unroll=True)
             corr[0:tokens, lane : lane + LANES] = corr_lane[lane // LANES]
 
-    grad_now = grad_send[0]
-    for k, copy in enumerate(grad_rounds):
-        copy.wait_recv()
-        grad_now = grad_now + grad_recv[k]
-        if k + 1 < len(grad_rounds):
-            grad_send[k + 1] = grad_now
-            grad_rounds[k + 1].start()
-
     out_rows(0, qg, q_out, tokens - HALO, tokens)
     corr[...] = corr[...] + bias[...] * g[...]
     branch[...] = corr[...] * value[...]
     out_rows(1, branch, k_out, 0, tokens)
     branch[...] = corr[...] * key[...]
     out_rows(2, branch, v_out, 0, tokens)
+    grad_now = next_grad_round(len(grad_rounds) - 1)
     scale = adapter_scale / math.sqrt(length)
     down_out[...] = grad_now[:rank] * scale
     up_out[...] = grad_now[rank:] * scale
@@ -500,20 +531,20 @@
     rank_rounds = n_tp.bit_length() - 1
     grad_rounds = n_ctx.bit_length() - 1
     vmem = pl.BlockSpec(memory_space=pltpu.VMEM)
-    anywhere = pl.BlockSpec(memory_space=pl.ANY)
+    hbm = pl.BlockSpec(memory_space=pltpu.HBM)
     buffer = pltpu.VMEM
     dma = pltpu.SemaphoreType.DMA
     pair = (2, tokens, half)
     outs = pl.pallas_call(
         functools.partial(kernel, n_ctx, n_tp, tokens * n_ctx),
         out_shape=(
-            jax.ShapeDtypeStruct((tokens, channels), bf16),
-            jax.ShapeDtypeStruct((tokens, channels), bf16),
-            jax.ShapeDtypeStruct((tokens, channels), bf16),
-            jax.ShapeDtypeStruct((rank, channels), f32),
-            jax.ShapeDtypeStruct((rank, features), f32),
+            buffer((tokens, channels), bf16),
+            buffer((tokens, channels), bf16),
+            buffer((tokens, channels), bf16),
+            buffer((rank, channels), f32),
+            buffer((rank, features), f32),
         ),
-        in_specs=[anywhere] * 6 + [vmem] * 6,
+        in_specs=[hbm] * 12,
         out_specs=(vmem,) * 5,
         scratch_shapes=[
             buffer((tokens, channels), bf16),
@@ -522,6 +553,12 @@
             buffer((tokens, channels), bf16),
             buffer((n_tp, channels, features), bf16),
             buffer((tokens, features), bf16),
+            buffer(short_conv_filter.shape, f32),
+            buffer((1, channels), f32),
+            buffer((modes, channels), f32),
+            buffer((modes, channels), f32),
+            buffer((rank, adapter_down_factor.shape[0]), bf16),
+            buffer((rank, features), bf16),
             buffer((3, HALO, channels), bf16),
             buffer((2, HALO, channels), bf16),
             buffer((tokens + 16, channels), f32),
@@ -538,8 +575,8 @@
             buffer(pair, bf16),
             buffer((rank_rounds, 2 * rank, tokens), f32),
             buffer((rank_rounds, 2 * rank, tokens), f32),
-            buffer((grad_rounds, 2 * rank, channels), f32),
-            buffer((grad_rounds, 2 * rank, channels), f32),
+            buffer((grad_rounds, 2 * rank, channels), bf16),
+            buffer((grad_rounds, 2 * rank, channels), bf16),
             buffer((tokens + 8, channels), f32),
             buffer((tokens + 8, channels), f32),
             buffer((tokens + 8, channels), f32),
@@ -551,9 +588,11 @@
             buffer((channels // LANES, SEGMENTS * modes, LANES), f32),
             buffer((SEGMENTS * modes, channels), f32),
             buffer((modes, channels), f32),
-            buffer((2, MESSAGE, half), f32),
-            buffer((n_ctx - 1, 2, MESSAGE, half), f32),
-            dma((5,)),
+            buffer((2, 2 * modes, half), bf16),
+            buffer((2, 2 * modes, half), bf16),
+            buffer((2, modes, half), bf16),
+            buffer((max(n_ctx - 2, 1), 2, modes, half), bf16),
+            dma((11,)),
             dma((n_tp,)),
             dma((5,)),
             dma((5,)),
@@ -571,7 +610,7 @@
             dma((n_ctx - 1, 2)),
         ],
         compiler_params=pltpu.CompilerParams(
-            collective_id=0, has_side_effects=True, vmem_limit_bytes=40 * 1024 * 1024
+            collective_id=0, has_side_effects=True, vmem_limit_bytes=62 * 1024 * 1024
         ),
     )(
         query_projected,

time: 39.5 us -> 25.3 us (0.64); the launches traced: 38.9 us -> 25.1 us
  local copies, waits for them, and re-layouts: 14 us -> 3.26 us
  Pallas kernels: 24.2 us -> 21.2 us
    unnamed x29 -> x5, local copies, waits for them, and re-layouts: 14 us -> 3.26 us
    pallas_call x1, Pallas kernels: 24.2 us -> 21.2 us  [on_device(): pl.pallas_call(functools.partial(kernel, n_ctx, n_tp, tokens * n_ctx), ou...]
where the time goes in v2:
time: 25.3 us; the launch traced here: 25.1 us
  Pallas kernels  21.2 us (84%)
  local copies, waits for them, and re-layouts  3.26 us (13%)
  between operations  0.65 us (3%)
    pallas_call x1, Pallas kernels, on_device(): pl.pallas_call(functools.partial(kernel, n_ctx, n_tp, tokens * n_ctx), ou...  21.2 us
    unnamed x5, local copies, waits for them, and re-layouts  3.26 us

profile of v2, /device:TPU:0, one launch (start us, length us, event | category | flops | bytes accessed | tf_op | source)
XLA Modules:
  0.0 25.1 jit_solution(12885087584211706048)
XLA Ops:
  0.6 21.2 %shard_map.155 = (bf16[192,512]{1,0:T(8,128)(2,1)S(1)}, bf16[192,512]{1,0:T(8,128)(2,1)S(1)}, bf16[192,512]{1,0:T(8,128)(2,1)S(1)}, f32[16,512]{1,0:T(8,128)S(1)}, f32[16,512]{1,0:T(8,128)S(1)}) custom-call(bf16[192,512]{1,0:T(8,128)(2,1)} %qp_any.1, bf16[192,512]{1,0:T(8,128)(2,1)} %kp_any.1, bf16[192,512]{1,0:T(8,128)(2,1)} %vp_any.1, ...), custom_call_target="tpu_custom_call" | custom-call | tf_op jit(solution)/shard_map/pallas_call | solution.py:538
  21.9 0.7 %copy.22 = bf16[192,512]{1,0:T(8,128)(2,1)} copy(bf16[192,512]{1,0:T(8,128)(2,1)S(1)} %get-tuple-element.15) | data formatting | bytes 393216
  22.5 0.6 %copy.25 = f32[512,16]{0,1:T(8,128)} copy(f32[512,16]{0,1:T(8,128)S(1)} %bitcast.5) | data formatting | bytes 65536
  23.2 0.6 %copy.26 = f32[16,512]{1,0:T(8,128)} copy(f32[16,512]{1,0:T(8,128)S(1)} %get-tuple-element.19) | data formatting | bytes 65536
  23.8 0.7 %copy.23 = bf16[192,512]{1,0:T(8,128)(2,1)} copy(bf16[192,512]{1,0:T(8,128)(2,1)S(1)} %get-tuple-element.16) | data formatting | bytes 393216
  24.5 0.7 %copy.24 = bf16[192,512]{1,0:T(8,128)(2,1)} copy(bf16[192,512]{1,0:T(8,128)(2,1)S(1)} %get-tuple-element.17) | data formatting | bytes 393216
